TPU v7x, 32 devices: a whole 2x2x4 slice. The times are simulated.
32 devices in a mesh: groups: 2 (over x), wide: 16 (over z, y, core).
Axes of the slice: x: 2, y: 2, z: 4, core: 2. Of those that a mesh axis runs over, the one named last changes fastest.
Arguments:
- picture_feature_maps: bfloat16 [256, 10, 10, 1536], P(('groups', 'wide')), parts along dimension 0, may hold values from -6 to 6
- partitioned_filter_tensor: bfloat16 [3, 3, 128, 1536], replicated, may hold values from -0.1875 to 0.1875
- picture_token_layer_scaling: float32 [1536], replicated, may hold values from 0.1 to 1.9
- summary_probes: bfloat16 [64, 1536], replicated, may hold values from -6 to 6
- summary_probe_layer_scaling: float32 [1536], replicated, may hold values from 0.1 to 1.9
- asking_projection_tensor: bfloat16 [1536, 1536], P('wide'), may hold values from -0.15625 to 0.15625
- lookup_projection_tensor: bfloat16 [1536, 1536], P('wide'), may hold values from -0.15625 to 0.15625
- content_projection_tensor: bfloat16 [1536, 1536], P('wide'), may hold values from -0.15625 to 0.15625
- final_projection_tensor: bfloat16 [1536, 1536], P(None, 'wide'), may hold values from -0.15625 to 0.15625
- sharpness_coefficient: float32 [16], replicated, may hold values from 0.5 to 64
Outputs:
- attended: float32 [128, 1536], P('groups'), parts along dimension 0
- new_latents: bfloat16 [128, 1536], P('groups'), parts along dimension 0
There are 2 independent parts, one for each index of `groups`. A program takes and returns all parts, laid end to end along the dimension named above; an argument that names none is the same for every part. Nothing has to cross between parts.
All inputs are finite; a program needn't handle non-finite values.
Results may differ from a plain program's by a relative error of at most 0.004.
The roundings to bfloat16 on the way count: a program that leaves them out, or rounds other values in their place, can miss the bound.
Values may be sent and summed in bfloat16 or wider, within the bound.
A program may use at most 128 MiB of HBM per device.

v0:
```python
import math
import jax
import jax.numpy as jnp
from jax import lax
from jax.sharding import PartitionSpec as P

RESIDUAL_SCALE = 0.2
EPSILON = 1e-06


def layer_norm(values, gain):
    center = values - jnp.mean(values, axis=-1, keepdims=True)
    spread = jnp.mean(center * center, axis=-1, keepdims=True)
    return center * lax.rsqrt(spread + EPSILON) * gain


def combine(left_side, right_side):
    left_max, left_sum, left_weighted = left_side
    right_max, right_sum, right_weighted = right_side
    joint_max = jnp.maximum(left_max, right_max)
    scale_left = jnp.exp(left_max - joint_max)
    scale_right = jnp.exp(right_max - joint_max)
    return (
        joint_max,
        left_sum * scale_left + right_sum * scale_right,
        left_weighted * scale_left[..., None] + right_weighted * scale_right[..., None],
    )


def merge_all(row_max, row_sum, weighted):
    joint_max = lax.pmax(row_max, "wide")
    factor = jnp.exp(row_max - joint_max)
    joint_sum, joint_weighted = lax.psum((row_sum * factor, weighted * factor[..., None]), "wide")
    return (joint_max, joint_sum, joint_weighted)


def softmax_terms(scores, carried):
    row_max = jnp.max(scores, axis=-1)
    weights = jnp.exp(scores - row_max[..., None])
    row_sum = jnp.sum(weights, axis=-1)
    weighted = jnp.einsum("hlt,thd->hld", weights, carried, precision=lax.Precision.HIGHEST)
    return (row_max, row_sum, weighted)


def per_device(
    picture_feature_maps,
    partitioned_filter_tensor,
    picture_token_layer_scaling,
    summary_probes,
    summary_probe_layer_scaling,
    asking_projection_tensor,
    lookup_projection_tensor,
    content_projection_tensor,
    final_projection_tensor,
    sharpness_coefficient,
):
    channels = picture_feature_maps.shape[3]
    subspace_number_overall = sharpness_coefficient.shape[0]
    subspace_breadth = channels // subspace_number_overall
    lat_count = summary_probes.shape[0]
    activated = jax.nn.gelu(picture_feature_maps.astype(jnp.float32)).astype(jnp.bfloat16)
    convolved = lax.conv_general_dilated(
        activated,
        partitioned_filter_tensor,
        (1, 1),
        "SAME",
        dimension_numbers=("NHWC", "HWIO", "NHWC"),
        feature_group_count=channels // partitioned_filter_tensor.shape[2],
        preferred_element_type=jnp.float32,
    )
    summed = picture_feature_maps.astype(jnp.float32) + RESIDUAL_SCALE * convolved
    tok_norm = layer_norm(summed.reshape(-1, channels), picture_token_layer_scaling).astype(
        jnp.bfloat16
    )
    lat_norm = layer_norm(summary_probes.astype(jnp.float32), summary_probe_layer_scaling).astype(
        jnp.bfloat16
    )
    tok_count = tok_norm.shape[0]
    shard_rows = asking_projection_tensor.shape[0]
    first_row = lax.axis_index("wide") * shard_rows
    lat_slice = lax.dynamic_slice_in_dim(lat_norm, first_row, shard_rows, 1)
    probe_asking_vectors = lax.psum(
        jnp.dot(lat_slice, asking_projection_tensor, preferred_element_type=jnp.float32), "wide"
    )
    rescaled_similarity_logits = (
        probe_asking_vectors.reshape(lat_count, subspace_number_overall, subspace_breadth)
        * (sharpness_coefficient / math.sqrt(subspace_breadth))[None, :, None]
    )
    key_source = jnp.concatenate([tok_norm, lat_norm], axis=0)
    zero_rows = jnp.zeros((key_source.shape[0], channels), jnp.float32)

    def add_rows(running, weight_rows):
        return running + jnp.dot(key_source, weight_rows, preferred_element_type=jnp.float32)

    def scores_of(key_part):
        return jnp.einsum(
            "lhd,thd->hlt",
            rescaled_similarity_logits,
            key_part.reshape(-1, subspace_number_overall, subspace_breadth),
            precision=lax.Precision.HIGHEST,
        )

    running = (zero_rows, zero_rows)
    weight_rows = (
        lax.all_gather(lookup_projection_tensor, "wide", axis=0, tiled=True),
        lax.all_gather(content_projection_tensor, "wide", axis=0, tiled=True),
    )
    key_proj = add_rows(running[0], weight_rows[0])
    value_proj = add_rows(running[1], weight_rows[1])
    tok_terms = softmax_terms(
        scores_of(key_proj[:tok_count]),
        value_proj[:tok_count].reshape(-1, subspace_number_overall, subspace_breadth),
    )
    lat_terms = softmax_terms(
        scores_of(key_proj[tok_count:]),
        value_proj[tok_count:].reshape(-1, subspace_number_overall, subspace_breadth),
    )
    merged = merge_all(*tok_terms)
    joint_max, joint_sum, joint_weighted = combine(merged, lat_terms)
    attention = (
        (joint_weighted / joint_sum[..., None]).transpose(1, 0, 2).reshape(lat_count, channels)
    )
    attention_low = attention.astype(jnp.bfloat16)
    out_cols = jnp.dot(attention_low, final_projection_tensor, preferred_element_type=jnp.float32)
    attended = lax.all_gather(out_cols, "wide", axis=1, tiled=True)
    new_latents = (summary_probes.astype(jnp.float32) + attended).astype(jnp.bfloat16)
    return (attended, new_latents)


def solution(mesh):
    placed = (
        P(("groups", "wide"), None, None, None),
        P(),
        P(),
        P(),
        P(),
        P("wide", None),
        P("wide", None),
        P("wide", None),
        P(None, "wide"),
        P(),
    )
    return jax.shard_map(
        per_device,
        mesh=mesh,
        in_specs=placed,
        out_specs=(P("groups", None), P("groups", None)),
        check_vma=False,
    )
```

profile of v0, /device:TPU:0, one launch (start us, length us, event | category | flops | bytes accessed | tf_op | source)
XLA Modules:
  0.0 424.6 jit_solution(6361989302038620171)
XLA Ops:
  7.2 0.7 all-gather.4.cloned.1.call-update
  8.0 0.7 all-gather.6.cloned.1.call-update
  8.7 1.1 convert_reduce_fusion
  9.8 1.2 fusion.34
  11.0 1.1 fusion.36
  12.5 1.0 copy.42
  13.5 6.2 %copy.43 = bf16[3,3,128,1536]{2,3,1,0:T(8,128)(2,1)} copy(bf16[3,3,128,1536]{3,2,1,0:T(8,128)(2,1)} %param.11) | data formatting | bytes 7077888 | tf_op args[1]
  19.7 9.5 %fusion.55 = (f32[8,10,10]{0,2,1:T(8,128)S(1)}, f32[8,10,10,1536]{3,0,2,1:T(8,128)}) fusion(bf16[3,3,128,12,128]{2,4,3,1,0:T(8,128)(2,1)} %bitcast.34, bf16[8,10,10,1536]{3,0,2,1:T(8,128)(2,1)S(1)} %copy-done.9), kind=kOutput, calls=%fused_computation.74 | convolution fusion | flops 2483453184 | bytes 10914944 | tf_op jit(solution)/shard_map/conv_general_dilated | solution.py:62
  29.5 8.7 %copy.44 = f32[8,10,10,1536]{3,2,1,0:T(8,128)} copy(f32[8,10,10,1536]{3,0,2,1:T(8,128)} %get-tuple-element.8) | data formatting | bytes 9830400 | tf_op jit(solution)/shard_map/add | solution.py:71
  38.2 0.6 multiply_reduce_fusion
  39.1 6.6 %reshape.83 = f32[800,1536]{1,0:T(8,128)} reshape(f32[8,10,10,1536]{3,2,1,0:T(8,128)} %copy.44) | data formatting | bytes 9830400 | tf_op jit(solution)/shard_map/reshape | solution.py:72
  45.9 3.1 multiply_convert_fusion
  49.0 17.4 %all-gather.4.cloned.1.call-done = bf16[1536,1536]{1,0:T(8,128)(2,1)} async-done(((bf16[96,1536]{1,0:T(8,128)(2,1)}), bf16[1536,1536]{1,0:T(8,128)(2,1)}) %all-gather.4.cloned.1.call-update) | async-done | bytes 4718608 | tf_op jit(solution)/shard_map/all_gather | solution.py:105
  66.4 8.6 %fusion.19 = f32[864,1536]{1,0:T(8,128)} fusion(bf16[1536,1536]{1,0:T(8,128)(2,1)} %all-gather.4.cloned.1.call-done, bf16[64,1536]{1,0:T(8,128)(2,1)S(1)} %fusion.36, bf16[800,1536]{1,0:T(8,128)(2,1)S(1)} %multiply_convert_fusion), kind=kOutput, calls=%fused_computation.25 | convolution fusion | flops 4082171904 | bytes 12681216 | tf_op jit(solution)/shard_map/dot_general | solution.py:93
  75.0 45.7 %all-gather.6.cloned.1.call-done = bf16[1536,1536]{1,0:T(8,128)(2,1)} async-done(((bf16[96,1536]{1,0:T(8,128)(2,1)}), bf16[1536,1536]{1,0:T(8,128)(2,1)}) %all-gather.6.cloned.1.call-update) | async-done | bytes 4718608 | tf_op jit(solution)/shard_map/all_gather | solution.py:106
  120.7 6.5 %fusion.18 = f32[864,1536]{1,0:T(8,128)S(1)} fusion(bf16[1536,1536]{1,0:T(8,128)(2,1)} %all-gather.6.cloned.1.call-done, bf16[64,1536]{1,0:T(8,128)(2,1)S(1)} %fusion.36, bf16[800,1536]{1,0:T(8,128)(2,1)S(1)} %multiply_convert_fusion), kind=kOutput, calls=%fused_computation.24 | convolution fusion | flops 4082171904 | bytes 12681216 | tf_op jit(solution)/shard_map/dot_general | solution.py:93
  127.2 2.8 slice.16
  130.0 2.5 slice.17
  132.5 6.0 %copy.50 = f32[800,1536]{0,1:T(8,128)} copy(f32[800,1536]{1,0:T(8,128)} %slice.16) | data formatting | bytes 9830400 | tf_op jit(solution)/shard_map/slice | solution.py:111
  138.5 74.2 %all-reduce.3.cloned.1.call-done = f32[64,16,96]{2,0,1:T(8,128)} async-done(((f32[64,16,96]{2,0,1:T(8,128)}), f32[64,16,96]{2,0,1:T(8,128)}) %all-reduce.3.cloned.1.call-update) | async-done | bytes 393232 | tf_op jit(solution)/shard_map/psum | solution.py:82
  212.7 8.3 %fusion.56 = (f32[16,64]{1,0:T(8,128)S(1)}, f32[16,64,800]{2,1,0:T(8,128)}) fusion(f32[800,16,96]{0,2,1:T(8,128)} %bitcast.30, f32[64,16,96]{2,0,1:T(8,128)} %all-reduce.3.cloned.1.call-done, f32[16]{0:T(128)S(1)} %broadcast_multiply_fusion.1), kind=kOutput, calls=%fused_computation.75 | convolution fusion | flops 944634880 | bytes 8589376 | tf_op jit(solution)/shard_map/lhd,thd->hlt/dot_general | solution.py:96
  221.0 32.4 %pmax.7 = f32[16,64]{1,0:T(8,128)S(1)} all-reduce(f32[16,64]{1,0:T(8,128)S(1)} %get-tuple-element.9), channel_id=1, replica_groups=mesh['groups'=2,'wide'=16] {'wide'}, use_global_device_ids=true, to_apply=%region_6.0 | all-reduce | flops 1024 | bytes 8192 | tf_op jit(solution)/shard_map/pmax | solution.py:31
  253.5 2.9 fusion.6
  256.4 30.0 %psum.23 = f32[16,64]{1,0:T(8,128)S(1)} all-reduce(f32[16,64]{1,0:T(8,128)S(1)} %get-tuple-element.5), channel_id=1, replica_groups=mesh['groups'=2,'wide'=16] {'wide'}, use_global_device_ids=true, to_apply=%region_10.0 | all-reduce | flops 1024 | bytes 8192 | tf_op jit(solution)/shard_map/psum | solution.py:33
  286.6 6.0 %copy.51 = f32[800,1536]{0,1:T(8,128)} copy(f32[800,1536]{1,0:T(8,128)} %slice.17) | data formatting | bytes 9830400 | tf_op jit(solution)/shard_map/slice | solution.py:112
  292.6 11.3 %fusion.20 = f32[16,64,96]{2,1,0:T(8,128)} fusion(f32[800,16,96]{0,2,1:T(8,128)} %bitcast.31, f32[16,64,800]{2,1,0:T(8,128)} %get-tuple-element.10, f32[16,64]{1,0:T(8,128)S(1)} %get-tuple-element.9, f32[16,64]{1,0:T(8,128)S(1)} %get-tuple-element.6), kind=kOutput, calls=%fused_computation.26 | convolution fusion | flops 944635904 | bytes 8593408 | tf_op jit(solution)/shard_map/hlt,thd->hld/dot_general | solution.py:41
  304.1 1.1 fusion.57
  305.4 85.9 %all-reduce.5.cloned.1.call-done = f32[16,64,96]{2,1,0:T(8,128)} async-done(((f32[16,64,96]{2,1,0:T(8,128)}), f32[16,64,96]{2,1,0:T(8,128)}) %all-reduce.5.cloned.1.call-update) | async-done | bytes 393232 | tf_op jit(solution)/shard_map/psum | solution.py:33
  391.3 2.5 fusion.24
  394.4 22.2 %all-gather = f32[16,96,64]{1,2,0:T(8,128)S(1)} all-gather(f32[1,96,64]{1,2,0:T(8,128)S(1)} %convolution_bitcast_fusion), channel_id=1, replica_groups=mesh['groups'=2,'wide'=16] {'wide'}, dimensions={0}, use_global_device_ids=true | all-gather | bytes 417792 | tf_op jit(solution)/shard_map/all_gather | solution.py:125
  416.7 0.3 copy.56
  417.2 0.8 fusion.37
  (60 shorter events, 2.8 us)
Async XLA Ops:
  7.2 4.9 %copy-start = (bf16[96,1536]{1,0:T(8,128)(2,1)S(1)}, bf16[96,1536]{1,0:T(8,128)(2,1)}, u32[]{:S(2)}) copy-start(bf16[96,1536]{1,0:T(8,128)(2,1)} %param.15) | copy-start | bytes 884740
  7.2 59.2 %all-gather.4.cloned.1.call-start = ((), (), s32[]{:S(2)}) async-start(), calls=%async_computation.1 | async-start | bytes 5013504 | tf_op jit(solution)/shard_map/all_gather | solution.py:105
  7.9 112.8 %all-gather.6.cloned.1.call-start = ((), (), s32[]{:S(2)}) async-start(), calls=%async_computation.2 | async-start | bytes 5013504 | tf_op jit(solution)/shard_map/all_gather | solution.py:106
  8.7 204.1 %all-reduce.3.cloned.1.call-start = ((), (), s32[]{:S(2)}) async-start(), calls=%async_computation | async-start | bytes 1048576 | tf_op jit(solution)/shard_map/psum | solution.py:82
  13.5 6.3 %copy-start.9 = (bf16[8,10,10,1536]{3,0,2,1:T(8,128)(2,1)S(1)}, bf16[8,10,10,1536]{3,0,2,1:T(8,128)(2,1)}, u32[]{:S(2)}) copy-start(bf16[8,10,10,1536]{3,0,2,1:T(8,128)(2,1)} %param.10) | copy-start | bytes 7372804
  13.5 377.8 %all-reduce.5.cloned.1.call-start = ((), (), s32[]{:S(2)}) async-start(), calls=%async_computation.3 | async-start | bytes 1048576 | tf_op jit(solution)/shard_map/psum | solution.py:33
  29.3 8.8 %slice-start = ((s8[4915200]{0:T(1024)(128)(4,1)}), s8[720896]{0:T(1024)(128)(4,1)S(1)}, s32[]{:S(2)}) async-start(s8[4915200]{0:T(1024)(128)(4,1)} %bitcast.32), calls=%async_computation.4 | async-start | bytes 1441792
  29.5 8.7 %slice-start.1 = ((s8[4915200]{0:T(1024)(128)(4,1)}), s8[4194304]{0:T(1024)(128)(4,1)S(1)}, s32[]{:S(2)}) async-start(s8[4915200]{0:T(1024)(128)(4,1)} %bitcast.32), calls=%async_computation.5 | async-start | bytes 8388608
  39.1 6.8 %copy-start.10 = (f32[16]{0:T(128)S(1)}, f32[16]{0:T(128)}, u32[]{:S(2)}) copy-start(f32[16]{0:T(128)} %param.19) | copy-start | bytes 196
  39.1 6.8 %copy-start.8 = (f32[1536]{0:T(1024)S(1)}, f32[1536]{0:T(1024)}, u32[]{:S(2)}) copy-start(f32[1536]{0:T(1024)} %param.12) | copy-start | bytes 18436
  120.7 6.5 %copy-start.2 = (f32[864,1536]{1,0:T(8,128)S(1)}, f32[864,1536]{1,0:T(8,128)}, u32[]{:S(2)}) copy-start(f32[864,1536]{1,0:T(8,128)} %fusion.19) | copy-start | bytes 15925252
  127.2 5.4 %copy-start.3 = (f32[864,1536]{1,0:T(8,128)}, f32[864,1536]{1,0:T(8,128)S(1)}, u32[]{:S(2)}) copy-start(f32[864,1536]{1,0:T(8,128)S(1)} %fusion.18) | copy-start | bytes 15925252
  212.7 73.7 %slice-start.2 = ((f32[864,1536]{1,0:T(8,128)}), f32[64,1536]{1,0:T(8,128)S(1)}, s32[]{:S(2)}) async-start(f32[864,1536]{1,0:T(8,128)} %fusion.19), calls=%async_computation.6 | async-start | bytes 786432 | tf_op jit(solution)/shard_map/slice | solution.py:115
  292.5 11.3 %slice-start.3 = ((f32[864,1536]{1,0:T(8,128)}), f32[64,1536]{1,0:T(8,128)S(1)}, s32[]{:S(2)}) async-start(f32[864,1536]{1,0:T(8,128)} %copy-done.3), calls=%async_computation.7 | async-start | bytes 786432 | tf_op jit(solution)/shard_map/slice | solution.py:116
  292.6 11.5 %copy-start.5 = (f32[64,16,96]{2,0,1:T(8,128)S(1)}, f32[64,16,96]{2,0,1:T(8,128)}, u32[]{:S(2)}) copy-start(f32[64,16,96]{2,0,1:T(8,128)} %all-reduce.3.cloned.1.call-done) | copy-start | bytes 1179652
  303.8 90.4 %copy-start.7 = (bf16[1536,96]{0,1:T(8,128)(2,1)S(1)}, bf16[1536,96]{0,1:T(8,128)(2,1)}, u32[]{:S(2)}) copy-start(bf16[1536,96]{0,1:T(8,128)(2,1)} %param.18) | copy-start | bytes 884740
  303.9 113.4 %copy-start.4 = (bf16[64,1536]{1,0:T(8,128)(2,1)S(1)}, bf16[64,1536]{1,0:T(8,128)(2,1)}, u32[]{:S(2)}) copy-start(bf16[64,1536]{1,0:T(8,128)(2,1)} %param.13) | copy-start | bytes 589828
  303.9 114.2 %copy-start.1 = (bf16[96,1536]{1,0:T(8,128)(2,1)S(1)}, bf16[96,1536]{1,0:T(8,128)(2,1)}, u32[]{:S(2)}) copy-start(bf16[96,1536]{1,0:T(8,128)(2,1)} %param.15) | copy-start | bytes 884740
  417.2 0.8 copy-start.6
Sparse Core Ops, SparseCore 0:
  10.3 56.0 all-gather.3
  68.7 51.9 all-gather.5
  124.1 88.5 all-reduce.2
  304.0 87.2 all-reduce.4
where the time goes:
time: 425 us
  waiting for transfers between devices  225 us (53%)
  blocking collectives  84.7 us (20%)
  matrix products  48.2 us (11%)
  local copies, waits for them, and re-layouts  42 us (10%)
  between operations  14.1 us (3%)
  other arithmetic  10.9 us (3%)
    psum x1, waiting for transfers between devices, merge_all(): lax.psum((row_sum * factor, weighted * factor[..., None]), 'wide')  85.9 us
    psum x1, waiting for transfers between devices, per_device(): lax.psum(jnp.dot(lat_slice, asking_projection_tensor, preferred_element_t...  74.2 us
    all_gather x1, waiting for transfers between devices, per_device(): lax.all_gather(content_projection_tensor, 'wide', axis=0, tiled=True)  45.7 us
    pmax x1, blocking collectives, merge_all(): joint_max = lax.pmax(row_max, 'wide')  32.4 us
    psum x1, blocking collectives, merge_all(): lax.psum((row_sum * factor, weighted * factor[..., None]), 'wide')  30 us
    all_gather x1, blocking collectives, per_device(): attended = lax.all_gather(out_cols, 'wide', axis=1, tiled=True)  22.2 us
    all_gather x1, waiting for transfers between devices, per_device(): lax.all_gather(lookup_projection_tensor, 'wide', axis=0, tiled=True)  17.4 us
    dot_general x2, matrix products, add_rows(): jnp.dot(key_source, weight_rows, preferred_element_type=jnp.float32)  15 us
  transfers between devices with their start and end apart: 4, of which 4 were waited for; matrix products, arithmetic and copies ran while one was open for 16% of the time, Pallas kernels for 0%

commit v1 on v0

--- a/solution.py
+++ b/solution.py
@@ -6,6 +6,18 @@
 
 RESIDUAL_SCALE = 0.2
 EPSILON = 1e-06
+
+
+def gather_by_bits(x, axis, dim):
+    ways, here = (lax.axis_size(axis), lax.axis_index(axis))
+    grown, reach = (x, 1)
+    while reach < ways:
+        theirs = lax.ppermute(grown, axis, [(d, d ^ reach) for d in range(ways)])
+        mine_first = jnp.concatenate([grown, theirs], axis=dim)
+        theirs_first = jnp.concatenate([theirs, grown], axis=dim)
+        grown = jnp.where(here & reach == 0, mine_first, theirs_first)
+        reach = 2 * reach
+    return grown
 
 
 def layer_norm(values, gain):
@@ -102,7 +114,7 @@
 
     running = (zero_rows, zero_rows)
     weight_rows = (
-        lax.all_gather(lookup_projection_tensor, "wide", axis=0, tiled=True),
+        gather_by_bits(lookup_projection_tensor, "wide", 0),
         lax.all_gather(content_projection_tensor, "wide", axis=0, tiled=True),
     )
     key_proj = add_rows(running[0], weight_rows[0])

time: 425 us -> 418 us (0.984)
  waiting for transfers between devices: 225 us -> 201 us
  starting transfers between devices: 0.16 us -> 7.91 us
    ppermute x0 -> x4, waiting for transfers between devices: none -> 113 us  [gather_by_bits(): theirs = lax.ppermute(grown, axis, [(d, d ^ reach) for d in range(ways)])]
    psum x1, waiting for transfers between devices: 74.2 us -> 0.01 us  [per_device(): lax.psum(jnp.dot(lat_slice, asking_projection_tensor, preferred_element_t...]
    all_gather x1, waiting for transfers between devices: 45.7 us -> 0.02 us  [per_device(): lax.all_gather(content_projection_tensor, 'wide', axis=0, tiled=True)]
    all_gather x1 -> x0, waiting for transfers between devices: 17.4 us -> none  [per_device(): lax.all_gather(lookup_projection_tensor, 'wide', axis=0, tiled=True)]
    ppermute x0 -> x4, starting transfers between devices: none -> 7.79 us  [gather_by_bits(): theirs = lax.ppermute(grown, axis, [(d, d ^ reach) for d in range(ways)])]
    unnamed x28 -> x30, local copies, waits for them, and re-layouts: 6.53 us -> 9.49 us
  transfers between devices with their start and end apart: 4 -> 7, of which waited for: 4 -> 5; matrix products, arithmetic and copies ran while one was open for 16% -> 17% of each run, Pallas kernels for 0% -> 0%
where the time goes in v1:
time: 418 us
  waiting for transfers between devices  201 us (48%)
  blocking collectives  86.3 us (21%)
  matrix products  47.6 us (11%)
  local copies, waits for them, and re-layouts  46.2 us (11%)
  other arithmetic  14.2 us (3%)
  between operations  14.1 us (3%)
  starting transfers between devices  7.91 us (2%)
    ppermute x4, waiting for transfers between devices, gather_by_bits(): theirs = lax.ppermute(grown, axis, [(d, d ^ reach) for d in range(ways)])  113 us
    psum x1, waiting for transfers between devices, merge_all(): lax.psum((row_sum * factor, weighted * factor[..., None]), 'wide')  87.2 us
    pmax x1, blocking collectives, merge_all(): joint_max = lax.pmax(row_max, 'wide')  34 us
    psum x1, blocking collectives, merge_all(): lax.psum((row_sum * factor, weighted * factor[..., None]), 'wide')  30 us
    all_gather x1, blocking collectives, per_device(): attended = lax.all_gather(out_cols, 'wide', axis=1, tiled=True)  22.2 us
    dot_general x2, matrix products, softmax_terms(): jnp.einsum('hlt,thd->hld', weights, carried, precision=lax.Precision.HIGH...  13.7 us
    dot_general x2, matrix products, add_rows(): jnp.dot(key_source, weight_rows, preferred_element_type=jnp.float32)  13.3 us
    dot_general x2, matrix products, scores_of(): jnp.einsum('lhd,thd->hlt', rescaled_similarity_logits, key_part.reshape(-...  10.5 us
  transfers between devices with their start and end apart: 7, of which 5 were waited for; matrix products, arithmetic and copies ran while one was open for 17% of the time, Pallas kernels for 0%

profile of v1, /device:TPU:0, one launch (start us, length us, event | category | flops | bytes accessed | tf_op | source)
XLA Modules:
  0.0 417.7 jit_solution(4824030671447283107)
XLA Ops:
  7.2 1.1 convert_reduce_fusion
  8.3 1.2 fusion.40
  13.3 1.4 collective-permute-done
  14.7 1.2 maximum_select_fusion.4
  15.9 3.0 collective-permute-start.1
  18.9 15.2 %collective-permute-done.1 = bf16[192,1536]{1,0:T(8,128)(2,1)S(1)} collective-permute-done((bf16[192,1536]{1,0:T(8,128)(2,1)S(1)}, bf16[192,1536]{1,0:T(8,128)(2,1)S(1)}, u32[]{:S(2)}, u32[]{:S(2)}) %collective-permute-start.1) | collective-permute-done | bytes 589856 | tf_op jit(solution)/shard_map/ppermute | solution.py:15
  34.5 1.9 collective-permute-start.2
  36.3 6.0 %copy.43 = bf16[3,3,128,1536]{2,3,1,0:T(8,128)(2,1)} copy(bf16[3,3,128,1536]{3,2,1,0:T(8,128)(2,1)} %param.11) | data formatting | bytes 7077888 | tf_op args[1]
  42.4 21.4 %collective-permute-done.2 = bf16[384,1536]{1,0:T(8,128)(2,1)S(1)} collective-permute-done((bf16[384,1536]{1,0:T(8,128)(2,1)S(1)}, bf16[384,1536]{1,0:T(8,128)(2,1)S(1)}, u32[]{:S(2)}, u32[]{:S(2)}) %collective-permute-start.2) | collective-permute-done | bytes 1179680 | tf_op jit(solution)/shard_map/ppermute | solution.py:15
  63.8 1.8 maximum_select_fusion.2
  65.6 2.5 collective-permute-start.3
  68.0 9.7 %fusion.61 = (f32[8,10,10]{0,2,1:T(8,128)S(1)}, f32[8,10,10,1536]{3,0,2,1:T(8,128)}) fusion(bf16[3,3,128,12,128]{2,4,3,1,0:T(8,128)(2,1)S(1)} %bitcast.33, bf16[8,10,10,1536]{3,0,2,1:T(8,128)(2,1)} %param.10), kind=kOutput, calls=%fused_computation.84 | convolution fusion | flops 2483453184 | bytes 10914944 | tf_op jit(solution)/shard_map/conv_general_dilated | solution.py:74
  78.0 8.7 %copy.44 = f32[8,10,10,1536]{3,2,1,0:T(8,128)} copy(f32[8,10,10,1536]{3,0,2,1:T(8,128)} %get-tuple-element.8) | data formatting | bytes 9830400 | tf_op jit(solution)/shard_map/add | solution.py:83
  87.7 7.2 %reshape.83 = f32[800,1536]{1,0:T(8,128)} reshape(f32[8,10,10,1536]{3,2,1,0:T(8,128)} %copy.44) | data formatting | bytes 9830400 | tf_op jit(solution)/shard_map/reshape | solution.py:84
  95.0 3.1 multiply_convert_fusion
  98.1 75.3 %collective-permute-done.3 = bf16[768,1536]{1,0:T(8,128)(2,1)} collective-permute-done((bf16[768,1536]{1,0:T(8,128)(2,1)}, bf16[768,1536]{1,0:T(8,128)(2,1)}, u32[]{:S(2)}, u32[]{:S(2)}) %collective-permute-start.3) | collective-permute-done | bytes 2359328 | tf_op jit(solution)/shard_map/ppermute | solution.py:15
  173.5 7.1 %fusion.6 = f32[864,1536]{1,0:T(8,128)S(1)} fusion(bf16[768,1536]{1,0:T(8,128)(2,1)} %collective-permute-done.3, bf16[768,1536]{1,0:T(8,128)(2,1)} %maximum_select_fusion.2, pred[]{:T(512)S(6)} %eq.12, bf16[64,1536]{1,0:T(8,128)(2,1)S(1)} %fusion.42, bf16[800,1536]{1,0:T(8,128)(2,1)S(1)} %multiply_convert_fusion), kind=kOutput, calls=%fused_computation.14 | convolution fusion | flops 4103405568 | bytes 12681217 | tf_op jit(solution)/shard_map/dot_general | solution.py:105
  180.6 2.6 slice.16
  184.2 6.0 %copy.50 = f32[800,1536]{0,1:T(8,128)} copy(f32[800,1536]{1,0:T(8,128)} %slice.16) | data formatting | bytes 9830400 | tf_op jit(solution)/shard_map/slice | solution.py:123
  190.2 8.3 %fusion.62 = (f32[16,64]{1,0:T(8,128)S(1)}, f32[16,64,800]{2,1,0:T(8,128)}) fusion(f32[800,16,96]{0,2,1:T(8,128)} %bitcast.29, f32[64,16,96]{2,0,1:T(8,128)} %all-reduce.3.cloned.1.call-done, f32[16]{0:T(128)S(1)} %broadcast_multiply_fusion.1), kind=kOutput, calls=%fused_computation.85 | convolution fusion | flops 944634880 | bytes 8589376 | tf_op jit(solution)/shard_map/lhd,thd->hlt/dot_general | solution.py:108
  198.5 34.0 %pmax.7 = f32[16,64]{1,0:T(8,128)S(1)} all-reduce(f32[16,64]{1,0:T(8,128)S(1)} %get-tuple-element.9), channel_id=1, replica_groups=mesh['groups'=2,'wide'=16] {'wide'}, use_global_device_ids=true, to_apply=%region_6.7 | all-reduce | flops 1024 | bytes 8192 | tf_op jit(solution)/shard_map/pmax | solution.py:43
  232.6 2.9 fusion.13
  235.5 30.0 %psum.23 = f32[16,64]{1,0:T(8,128)S(1)} all-reduce(f32[16,64]{1,0:T(8,128)S(1)} %get-tuple-element.5), channel_id=1, replica_groups=mesh['groups'=2,'wide'=16] {'wide'}, use_global_device_ids=true, to_apply=%region_10.11 | all-reduce | flops 1024 | bytes 8192 | tf_op jit(solution)/shard_map/psum | solution.py:45
  265.5 2.2 fusion.63
  268.6 6.1 %fusion.25 = f32[864,1536]{1,0:T(8,128)S(1)} fusion(bf16[1536,1536]{1,0:T(8,128)(2,1)} %all-gather.3.cloned.1.call-done, bf16[64,1536]{1,0:T(8,128)(2,1)S(1)} %fusion.42, bf16[800,1536]{1,0:T(8,128)(2,1)S(1)} %multiply_convert_fusion), kind=kOutput, calls=%fused_computation.33 | convolution fusion | flops 4082171904 | bytes 12681216 | tf_op jit(solution)/shard_map/dot_general | solution.py:105
  274.8 2.4 copy-done.2
  277.2 2.6 slice.17
  279.8 5.9 %copy.51 = f32[800,1536]{0,1:T(8,128)} copy(f32[800,1536]{1,0:T(8,128)} %slice.17) | data formatting | bytes 9830400 | tf_op jit(solution)/shard_map/slice | solution.py:124
  285.7 11.2 %fusion.26 = f32[16,64,96]{2,1,0:T(8,128)} fusion(f32[800,16,96]{0,2,1:T(8,128)} %bitcast.30, f32[16,64,800]{2,1,0:T(8,128)} %get-tuple-element.10, f32[16,64]{1,0:T(8,128)S(1)} %get-tuple-element.9, f32[16,64]{1,0:T(8,128)S(1)} %get-tuple-element.6), kind=kOutput, calls=%fused_computation.34 | convolution fusion | flops 944635904 | bytes 8593408 | tf_op jit(solution)/shard_map/hlt,thd->hld/dot_general | solution.py:53
  297.2 87.2 %all-reduce.5.cloned.1.call-done = f32[16,64,96]{2,1,0:T(8,128)} async-done(((f32[16,64,96]{2,1,0:T(8,128)}), f32[16,64,96]{2,1,0:T(8,128)}) %all-reduce.5.cloned.1.call-update) | async-done | bytes 393232 | tf_op jit(solution)/shard_map/psum | solution.py:45
  384.4 2.5 fusion.30
  387.5 22.2 %all-gather = f32[16,96,64]{1,2,0:T(8,128)S(1)} all-gather(f32[1,96,64]{1,2,0:T(8,128)S(1)} %convolution_bitcast_fusion), channel_id=1, replica_groups=mesh['groups'=2,'wide'=16] {'wide'}, dimensions={0}, use_global_device_ids=true | all-gather | bytes 417792 | tf_op jit(solution)/shard_map/all_gather | solution.py:137
  (69 shorter events, 9.7 us)
Async XLA Ops:
  7.2 3.4 copy-start
  7.2 183.0 %all-reduce.3.cloned.1.call-start = ((), (), s32[]{:S(2)}) async-start(), calls=%async_computation | async-start | bytes 1048576 | tf_op jit(solution)/shard_map/psum | solution.py:94
  12.0 256.6 %all-gather.3.cloned.1.call-start = ((), (), s32[]{:S(2)}) async-start(), calls=%async_computation.1 | async-start | bytes 5013504 | tf_op jit(solution)/shard_map/all_gather | solution.py:118
  12.8 371.6 %all-reduce.5.cloned.1.call-start = ((), (), s32[]{:S(2)}) async-start(), calls=%async_computation.2 | async-start | bytes 1048576 | tf_op jit(solution)/shard_map/psum | solution.py:45
  12.8 1.9 collective-permute-start
  15.9 18.2 %collective-permute-start.1 = (bf16[192,1536]{1,0:T(8,128)(2,1)S(1)}, bf16[192,1536]{1,0:T(8,128)(2,1)S(1)}, u32[]{:S(2)}, u32[]{:S(2)}) collective-permute-start(bf16[192,1536]{1,0:T(8,128)(2,1)S(1)} %maximum_select_fusion.4), channel_id=1, source_target_pairs={{0,2},{1,3},{2,0},{3,1},{4,6},{5,7},{6,4},{7,5},{8,10},{9,11},{10,... | collective-permute-start | bytes 1769480 | tf_op jit(solution)/shard_map/ppermute | solution.py:15
  34.5 29.3 %collective-permute-start.2 = (bf16[384,1536]{1,0:T(8,128)(2,1)S(1)}, bf16[384,1536]{1,0:T(8,128)(2,1)S(1)}, u32[]{:S(2)}, u32[]{:S(2)}) collective-permute-start(bf16[384,1536]{1,0:T(8,128)(2,1)S(1)} %maximum_select_fusion.3), channel_id=1, source_target_pairs={{0,4},{1,5},{2,6},{3,7},{4,0},{5,1},{6,2},{7,3},{8,12},{9,13},{10,... | collective-permute-start | bytes 3538952 | tf_op jit(solution)/shard_map/ppermute | solution.py:15
  42.4 25.7 %copy-start.3 = (bf16[3,3,128,1536]{2,3,1,0:T(8,128)(2,1)S(1)}, bf16[3,3,128,1536]{2,3,1,0:T(8,128)(2,1)}, u32[]{:S(2)}) copy-start(bf16[3,3,128,1536]{2,3,1,0:T(8,128)(2,1)} %copy.43) | copy-start | bytes 10616836
  65.6 107.9 %collective-permute-start.3 = (bf16[768,1536]{1,0:T(8,128)(2,1)}, bf16[768,1536]{1,0:T(8,128)(2,1)}, u32[]{:S(2)}, u32[]{:S(2)}) collective-permute-start(bf16[768,1536]{1,0:T(8,128)(2,1)} %maximum_select_fusion.2), channel_id=1, source_target_pairs={{0,8},{1,9},{2,10},{3,11},{4,12},{5,13},{6,14},{7,15},{8,0},{9,1},... | collective-permute-start | bytes 7077896 | tf_op jit(solution)/shard_map/ppermute | solution.py:15
  77.9 8.8 %slice-start = ((s8[4915200]{0:T(1024)(128)(4,1)}), s8[720896]{0:T(1024)(128)(4,1)S(1)}, s32[]{:S(2)}) async-start(s8[4915200]{0:T(1024)(128)(4,1)} %bitcast.31), calls=%async_computation.3 | async-start | bytes 1441792
  78.0 8.7 %slice-start.1 = ((s8[4915200]{0:T(1024)(128)(4,1)}), s8[4194304]{0:T(1024)(128)(4,1)S(1)}, s32[]{:S(2)}) async-start(s8[4915200]{0:T(1024)(128)(4,1)} %bitcast.31), calls=%async_computation.4 | async-start | bytes 8388608
  87.6 7.4 %copy-start.11 = (f32[16]{0:T(128)S(1)}, f32[16]{0:T(128)}, u32[]{:S(2)}) copy-start(f32[16]{0:T(128)} %param.19) | copy-start | bytes 196
  87.6 7.4 %copy-start.10 = (f32[1536]{0:T(1024)S(1)}, f32[1536]{0:T(1024)}, u32[]{:S(2)}) copy-start(f32[1536]{0:T(1024)} %param.12) | copy-start | bytes 18436
  190.2 75.3 %copy-start.5 = (f32[64,16,96]{2,0,1:T(8,128)S(1)}, f32[64,16,96]{2,0,1:T(8,128)}, u32[]{:S(2)}) copy-start(f32[64,16,96]{2,0,1:T(8,128)} %all-reduce.3.cloned.1.call-done) | copy-start | bytes 1179652
  267.7 0.8 copy-start.6
  274.8 2.4 copy-start.2
  285.7 11.3 %slice-start.2 = ((f32[864,1536]{1,0:T(8,128)}), f32[64,1536]{1,0:T(8,128)S(1)}, s32[]{:S(2)}) async-start(f32[864,1536]{1,0:T(8,128)} %copy-done.2), calls=%async_computation.5 | async-start | bytes 786432 | tf_op jit(solution)/shard_map/slice | solution.py:128
  285.7 98.7 %copy-start.7 = (f32[16,64,64]{1,2,0:T(8,128)S(1)}, f32[16,64,64]{1,2,0:T(8,128)}, u32[]{:S(2)}) copy-start(f32[16,64,64]{1,2,0:T(8,128)} %copy-done.6) | copy-start | bytes 786436
  297.0 90.3 %copy-start.9 = (bf16[1536,96]{0,1:T(8,128)(2,1)S(1)}, bf16[1536,96]{0,1:T(8,128)(2,1)}, u32[]{:S(2)}) copy-start(bf16[1536,96]{0,1:T(8,128)(2,1)} %param.18) | copy-start | bytes 884740
  297.0 113.3 %copy-start.4 = (bf16[64,1536]{1,0:T(8,128)(2,1)S(1)}, bf16[64,1536]{1,0:T(8,128)(2,1)}, u32[]{:S(2)}) copy-start(bf16[64,1536]{1,0:T(8,128)(2,1)} %param.13) | copy-start | bytes 589828
  297.0 114.1 %copy-start.1 = (bf16[96,1536]{1,0:T(8,128)(2,1)S(1)}, bf16[96,1536]{1,0:T(8,128)(2,1)}, u32[]{:S(2)}) copy-start(bf16[96,1536]{1,0:T(8,128)(2,1)} %param.15) | copy-start | bytes 884740
  410.3 0.8 copy-start.8
Sparse Core Ops, SparseCore 0:
  12.1 163.1 all-reduce.2
  177.6 53.6 all-gather.2
  297.1 87.2 all-reduce.4
